TPU v7x, 32 devices: a whole 2x2x4 slice. The times are simulated.
32 devices in a mesh: ctx: 32 (over z, y, x, core), seq: 1.
Axes of the slice: x: 2, y: 2, z: 4, core: 2. Of those that a mesh axis runs over, the one named last changes fastest.
Arguments:
- query_states: bfloat16 [4096, 4096], P(('seq', 'ctx')), may hold values from -6.5 to 6.5
- key_states: bfloat16 [4096, 512], P(('seq', 'ctx')), may hold values from -4 to 4
- value_states: bfloat16 [4096, 512], P(('seq', 'ctx')), may hold values from -4 to 4
- block_docs: int32 [32], P('seq'), may hold values from 0 to 3, never falling along the last dimension, each value on 1 to 12 neighbouring positions
Outputs:
- attended: bfloat16 [4096, 4096], P(('seq', 'ctx'))
Inputs may be any that keep to these rules, and one draw needn't show every extreme that they name: block_docs never falls along the sequence; every document covers 1 to min(12, 16) whole blocks, and some document covers exactly that many.
All inputs are finite; a program needn't handle non-finite values.
Results may differ from a plain program's by a relative error of at most 0.004.
Values may be sent and summed in bfloat16 or wider, within the bound.
No kernel may reach another device: no remote copies, remote signals or barrier semaphores. Data moves between devices by JAX's collectives and lax.ppermute only.
A program may use at most 64 MiB of HBM per device.

v0:
```python
import functools
import math

import jax
import jax.numpy as jnp
from jax import lax
from jax.experimental import pallas as pl
from jax.experimental.pallas import tpu as pltpu
from jax.sharding import PartitionSpec as P

HD = 128
BLK = 128
NEG = -1e30
LOW, HIGH = 1e-25, 1e35
EXP2_SCALE = math.log2(math.e) / math.sqrt(HD)
F32 = jnp.float32
BF16 = jnp.bfloat16
VMEM = pl.BlockSpec(memory_space=pltpu.VMEM)
HBM = pl.BlockSpec(memory_space=pltpu.HBM)
PARAMS = pltpu.CompilerParams(vmem_limit_bytes=40 * 1024 * 1024)


def dot_nt(a, b):
    return lax.dot_general(a, b, (((1,), (1,)), ((), ())), preferred_element_type=F32)


def dot_nn(a, b):
    return lax.dot_general(a, b, (((1,), (0,)), ((), ())), preferred_element_type=F32)


def cut(index, width=HD):
    return slice(index * width, (index + 1) * width)


def group_queries(q_ref, group, size):
    return jnp.concatenate([q_ref[:, cut(group * size + h)] for h in range(size)], axis=0)


def key_head(ref, group):
    return ref[:BLK, cut(group)]


def value_head(ref, group):
    return ref[BLK:, cut(group)]


def penalty(docs_ref, position, distance):
    source = position - distance
    same = docs_ref[jnp.maximum(source, 0)] == docs_ref[position]
    return jnp.where((source >= 0) & same, 0.0, -NEG).astype(F32)


def pack_kernel(k_hbm, v_hbm, kv_ref, sems):
    copies = [
        pltpu.make_async_copy(k_hbm, kv_ref.at[:BLK], sems.at[0]),
        pltpu.make_async_copy(v_hbm, kv_ref.at[BLK:], sems.at[1]),
    ]
    for copy in copies:
        copy.start()
    for copy in copies:
        copy.wait()


def own_kernel(groups, size, docs_hbm, q_hbm, kv_ref, out_ref, total_ref, pen_ref, q_ref, docs_ref, sems):
    copies = [pltpu.make_async_copy(docs_hbm, docs_ref, sems.at[groups])]
    for g in range(groups):
        at = cut(g, size * HD)
        copies.append(pltpu.make_async_copy(q_hbm.at[:, at], q_ref.at[:, at], sems.at[g]))
    for copy in copies[1:] + copies[:1]:
        copy.start()
    row = lax.broadcasted_iota(jnp.int32, (BLK, BLK), 0)
    col = lax.broadcasted_iota(jnp.int32, (BLK, BLK), 1)
    bias = jnp.concatenate([jnp.where(col <= row, 0.0, NEG).astype(F32)] * size, axis=0)
    for g in range(groups):
        copies[1 + g].wait()
        scores = dot_nt(group_queries(q_ref, g, size), key_head(kv_ref, g))
        weights = jnp.exp2(scores * EXP2_SCALE + bias)
        total_ref[g] = weights
        out_ref[g] = dot_nn(weights.astype(BF16), value_head(kv_ref, g))
    copies[0].wait()
    position = lax.axis_index("ctx")
    odd = lax.rem(position, 2)
    for i, distance in enumerate((2, 1, 3)):
        pen_ref[i] = jnp.full((8, HD), penalty(docs_ref, position, distance), F32)


def weigh(scores, pen):
    return jnp.exp2(scores * EXP2_SCALE - pen)


def add_blocks(queries, blocks, pens, group, out, total):
    scores = dot_nt(queries, jnp.concatenate([key_head(x, group) for x in blocks], axis=0))
    weights = [weigh(scores[:, cut(i)], pen) for i, pen in enumerate(pens)]
    rounded = jnp.concatenate([w.astype(BF16) for w in weights], axis=1)
    values = jnp.concatenate([value_head(x, group) for x in blocks], axis=0)
    return out + dot_nn(rounded, values), total + functools.reduce(jnp.add, weights)


def pick(pairs):
    odd = lax.rem(lax.axis_index("ctx"), 2) == 1
    return [jnp.where(odd, y[...], x[...]) for x, y in pairs]


def middle_kernel(groups, size, q_ref, pen_ref, even_a, odd_a, out_in, total_in, out_ref, total_ref):
    blocks = pick([(even_a, odd_a)])
    for g in range(groups):
        out_ref[g], total_ref[g] = add_blocks(
            group_queries(q_ref, g, size), blocks, [pen_ref[0][:1]], g, out_in[g], total_in[g]
        )


def last_kernel(
    groups, size, q_ref, pen_ref, out_in, total_in, even_b, odd_b, even_c, odd_c,
    own_ref, even_a, odd_a, out_hbm, out_ref, low_ref, high_ref, sems,
):
    copies = []
    for g in range(groups):
        at = cut(g, size * HD)
        copies.append(pltpu.make_async_copy(out_ref.at[:, at], out_hbm.at[:, at], sems.at[g]))

    def finish(g, out, total):
        row_total = jnp.sum(total, axis=1, keepdims=True)
        result = (out / row_total).astype(BF16)
        for h in range(size):
            out_ref[:, cut(g * size + h)] = result[cut(h, BLK)]
        copies[g].start()
        return row_total

    def extremes(row_totals):
        low = functools.reduce(jnp.minimum, row_totals)
        high = functools.reduce(jnp.maximum, row_totals)
        low_ref[0] = jnp.min(low)
        high_ref[0] = jnp.max(high)

    first = lax.axis_index("ctx") == 0

    @pl.when(first)
    def _():
        extremes([finish(g, out_in[g], total_in[g]) for g in range(groups)])

    @pl.when(jnp.logical_not(first))
    def _():
        blocks = pick([(even_b, odd_b), (even_c, odd_c)])
        pens = [pen_ref[1][:1], pen_ref[2][:1]]
        extremes([
            finish(g, *add_blocks(group_queries(q_ref, g, size), blocks, pens, g, out_in[g], total_in[g]))
            for g in range(groups)
        ])

    for copy in copies:
        copy.wait()
    safe = (low_ref[0] > LOW) & (high_ref[0] < HIGH)

    @pl.when(jnp.logical_not(safe))
    def _():
        blocks = [own_ref] + pick([(even_a, odd_a), (even_b, odd_b), (even_c, odd_c)])
        row = lax.broadcasted_iota(jnp.int32, (BLK, BLK), 0)
        col = lax.broadcasted_iota(jnp.int32, (BLK, BLK), 1)
        biases = [jnp.where(col <= row, 0.0, NEG).astype(F32)] + [-pen_ref[i][:1] for i in range(3)]
        for g in range(groups):

            def one_head(h, _):
                at = pl.ds(pl.multiple_of((g * size + h) * HD, HD), HD)
                queries = q_ref[:, at]
                scores = [dot_nt(queries, key_head(x, g)) + bias for x, bias in zip(blocks, biases)]
                top = functools.reduce(jnp.maximum, [jnp.max(x, axis=1, keepdims=True) for x in scores])
                weights = [jnp.exp2((x - top) * EXP2_SCALE) for x in scores]
                total = sum(jnp.sum(w, axis=1, keepdims=True) for w in weights)
                product = sum(dot_nn(w.astype(BF16), value_head(x, g)) for w, x in zip(weights, blocks))
                out_ref[:, at] = (product / total).astype(BF16)
                return 0

            lax.fori_loop(0, size, one_head, 0)
        store = pltpu.make_async_copy(out_ref, out_hbm, sems.at[0])
        store.start()
        store.wait()


def routes(n):
    step = n // 4
    forward = []
    for parity in (0, 1):
        route = {i: i + 2 for i in range(parity, n - 2, 2)}
        last = n - 2 + parity
        chain = [last, last ^ 1] + [(last ^ 1) - step * k for k in range(1, 4)] + [parity]
        route.update(zip(chain, chain[1:]))
        route.update({i: i ^ step for i in range(1 - parity, n, 2) if i not in route})
        forward.append(sorted(route.items()))
    across = {i: i + 3 for i in range(1, n - 3, 2)}
    for start, end in ((n - 3, 0), (n - 1, 2)):
        at = start
        for k in range(3):
            across[at] = start - step * (k + 1)
            at = across[at] - 1
        across[at] = end
    across.update({i: i + 1 for i in range(0, n, 2) if i not in across})
    swap = [(i, i ^ 1) for i in range(n)]
    return forward[0], forward[1], sorted(across.items()), swap


def in_hbm(array):
    return pltpu.with_memory_space_constraint(array, pltpu.HBM)


def after(value, *others):
    return lax.optimization_barrier((value, *others))[0]


def on_device(queries, keys, values, docs):
    row_count, width = keys.shape
    groups = width // HD
    size = queries.shape[1] // width
    rows = size * BLK
    n = lax.axis_size("ctx")
    assert row_count == BLK and n % 8 == 0
    even_on, odd_on, across, swap = routes(n)
    work = groups * rows * BLK * HD * 4
    cost = pl.CostEstimate(flops=0, bytes_accessed=0, transcendentals=0)
    packed = jax.ShapeDtypeStruct((2 * BLK, width), BF16)
    running = jax.ShapeDtypeStruct((groups, rows, HD), F32)
    dma = pltpu.SemaphoreType.DMA

    def move(block, route):
        return lax.ppermute(block, "ctx", route)

    def own(block):
        return pl.pallas_call(
            functools.partial(own_kernel, groups, size),
            out_shape=(running,) * 2 + (jax.ShapeDtypeStruct((3, 8, HD), F32), jax.ShapeDtypeStruct(queries.shape, BF16)),
            in_specs=[HBM, HBM, VMEM],
            out_specs=(VMEM,) * 4,
            scratch_shapes=[pltpu.SMEM(docs.shape, jnp.int32), dma((groups + 1,))],
            compiler_params=PARAMS,
            cost_estimate=cost,
            name="own_block",
        )(in_hbm(docs), in_hbm(queries), block)

    block = pl.pallas_call(
        pack_kernel,
        out_shape=packed,
        in_specs=[HBM, HBM],
        out_specs=VMEM,
        scratch_shapes=[dma((2,))],
        compiler_params=PARAMS,
        name="pack",
    )(in_hbm(keys), in_hbm(values))
    odd_a = move(block, odd_on)
    even_a = move(block, even_on)
    odd_b = move(block, swap)
    out, total, pen, local = own(block)
    even_c = move(after(block, pen), across)
    even_b = move(after(odd_a, pen), swap)
    odd_c = move(after(even_a, pen), swap)
    out, total = pl.pallas_call(
        functools.partial(middle_kernel, groups, size),
        out_shape=(running,) * 2,
        in_specs=[VMEM] * 6,
        out_specs=(VMEM,) * 2,
        input_output_aliases={4: 0, 5: 1},
        compiler_params=PARAMS,
        cost_estimate=cost,
        name="middle_block",
    )(local, pen, even_a, odd_a, out, total)
    return pl.pallas_call(
        functools.partial(last_kernel, groups, size),
        out_shape=jax.ShapeDtypeStruct(queries.shape, BF16),
        in_specs=[VMEM] * 11,
        out_specs=HBM,
        scratch_shapes=[
            pltpu.VMEM(queries.shape, BF16),
            pltpu.SMEM((1,), F32),
            pltpu.SMEM((1,), F32),
            dma((groups,)),
        ],
        compiler_params=PARAMS,
        cost_estimate=cost,
        name="last_blocks",
    )(local, pen, out, total, even_b, odd_b, even_c, odd_c, block, even_a, odd_a)


def solution(mesh):
    return jax.shard_map(
        on_device,
        mesh=mesh,
        in_specs=(
            P(("seq", "ctx"), None),
            P(("seq", "ctx"), None),
            P(("seq", "ctx"), None),
            P("seq"),
        ),
        out_specs=P(("seq", "ctx"), None),
        check_vma=False,
    )
```

profile of v0, /device:TPU:1, one launch (start us, length us, event | category | flops | bytes accessed | tf_op | source)
XLA Modules:
  0.0 32.9 jit_solution(16830700563836783088)
XLA Ops:
  0.0 1.0 %pack.1.kv_ref.own_ref = bf16[256,512]{1,0:T(8,128)(2,1)S(1)} custom-call(bf16[128,512]{1,0:T(8,128)(2,1)} %k_hbm.1, bf16[128,512]{1,0:T(8,128)(2,1)} %v_hbm.1), custom_call_target="tpu_custom_call" | custom-call | tf_op jit(solution)/shard_map/pack/pallas_call | solution.py:238
  1.0 2.1 %collective-permute-start.1 = (bf16[256,512]{1,0:T(8,128)(2,1)S(1)}, bf16[256,512]{1,0:T(8,128)(2,1)S(1)}, u32[]{:S(2)}, u32[]{:S(2)}) collective-permute-start(bf16[256,512]{1,0:T(8,128)(2,1)S(1)} %pack.1.kv_ref.own_ref), channel_id=1, source_target_pairs={{0,8},{1,3},{2,10},{3,5},{4,12},{5,7},{6,1},{7,9},{8,0},{9,11},{10... | collective-permute-start | bytes 786440 | tf_op jit(solution)/shard_map/ppermute | solution.py:224
  3.1 1.3 %collective-permute-start = (bf16[256,512]{1,0:T(8,128)(2,1)S(1)}, bf16[256,512]{1,0:T(8,128)(2,1)S(1)}, u32[]{:S(2)}, u32[]{:S(2)}) collective-permute-start(bf16[256,512]{1,0:T(8,128)(2,1)S(1)} %pack.1.kv_ref.own_ref), channel_id=1, source_target_pairs={{0,2},{1,9},{2,4},{3,11},{4,6},{5,13},{6,8},{7,0},{8,10},{9,1},{10... | collective-permute-start | bytes 786440 | tf_op jit(solution)/shard_map/ppermute | solution.py:224
  4.4 1.2 %collective-permute-start.3 = (bf16[256,512]{1,0:T(8,128)(2,1)S(1)}, bf16[256,512]{1,0:T(8,128)(2,1)S(1)}, u32[]{:S(2)}, u32[]{:S(2)}) collective-permute-start(bf16[256,512]{1,0:T(8,128)(2,1)S(1)} %pack.1.kv_ref.own_ref), channel_id=1, source_target_pairs={{0,1},{1,0},{2,3},{3,2},{4,5},{5,4},{6,7},{7,6},{8,9},{9,8},{10,11... | collective-permute-start | bytes 786440 | tf_op jit(solution)/shard_map/ppermute | solution.py:224
  5.6 2.7 %own_block.1 = (f32[4,1024,128]{2,1,0:T(8,128)S(1)}, f32[4,1024,128]{2,1,0:T(8,128)S(1)}, f32[3,8,128]{2,1,0:T(8,128)S(1)}, bf16[128,4096]{1,0:T(8,128)(2,1)S(1)}) custom-call(s32[32]{0:T(128)} %docs_hbm.1, bf16[128,4096]{1,0:T(8,128)(2,1)} %q_hbm.1, bf16[256,512]{1,0:T(8,128)(2,1)S(1)} %pack.1.kv_ref.own_ref), custom_call_target="tpu_custom_call" | custom-call | tf_op jit(solution)/shard_map/own_block/pallas_call | solution.py:227
  8.3 0.5 %collective-permute-start.4 = (bf16[256,512]{1,0:T(8,128)(2,1)S(1)}, bf16[256,512]{1,0:T(8,128)(2,1)S(1)}, u32[]{:S(2)}, u32[]{:S(2)}) collective-permute-start(bf16[256,512]{1,0:T(8,128)(2,1)S(1)} %pack.1.kv_ref.own_ref), channel_id=1, source_target_pairs={{0,1},{1,4},{2,3},{3,6},{4,0},{5,8},{6,2},{7,10},{8,9},{9,12},{10,... | collective-permute-start | bytes 786440 | tf_op jit(solution)/shard_map/ppermute | solution.py:224
  8.7 1.5 %collective-permute-done.1.odd_a = bf16[256,512]{1,0:T(8,128)(2,1)S(1)} collective-permute-done((bf16[256,512]{1,0:T(8,128)(2,1)S(1)}, bf16[256,512]{1,0:T(8,128)(2,1)S(1)}, u32[]{:S(2)}, u32[]{:S(2)}) %collective-permute-start.1) | collective-permute-done | bytes 262176 | tf_op jit(solution)/shard_map/ppermute | solution.py:224
  10.2 0.6 %collective-permute-start.2 = (bf16[256,512]{1,0:T(8,128)(2,1)S(1)}, bf16[256,512]{1,0:T(8,128)(2,1)S(1)}, u32[]{:S(2)}, u32[]{:S(2)}) collective-permute-start(bf16[256,512]{1,0:T(8,128)(2,1)S(1)} %collective-permute-done.1.odd_a), channel_id=1, source_target_pairs={{0,1},{1,0},{2,3},{3,2},{4,5},{5,4},{6,7},{7,6},{8,9},{9,8},{10,11... | collective-permute-start | bytes 786440 | tf_op jit(solution)/shard_map/ppermute | solution.py:224
  10.8 0.1 collective-permute-done.even_a
  10.9 1.3 %collective-permute-start.5 = (bf16[256,512]{1,0:T(8,128)(2,1)S(1)}, bf16[256,512]{1,0:T(8,128)(2,1)S(1)}, u32[]{:S(2)}, u32[]{:S(2)}) collective-permute-start(bf16[256,512]{1,0:T(8,128)(2,1)S(1)} %collective-permute-done.even_a), channel_id=1, source_target_pairs={{0,1},{1,0},{2,3},{3,2},{4,5},{5,4},{6,7},{7,6},{8,9},{9,8},{10,11... | collective-permute-start | bytes 786440 | tf_op jit(solution)/shard_map/ppermute | solution.py:224
  12.2 1.2 %middle_block.1 = (f32[4,1024,128]{2,1,0:T(8,128)S(1)}, f32[4,1024,128]{2,1,0:T(8,128)S(1)}) custom-call(bf16[128,4096]{1,0:T(8,128)(2,1)S(1)} %get-tuple-element.14.q_ref, f32[3,8,128]{2,1,0:T(8,128)S(1)} %get-tuple-element.15.pen_ref, bf16[256,512]{1,0:T(8,128)(2,1)S(1)} %collective-permute-done.even_a, ...), custom_call_target="tpu_custom_call", output_to_operand_aliasing={{0}: (4, {}), {1}: (5, {})} | custom-call | tf_op jit(solution)/shard_map/middle_block/pallas_call | solution.py:254
  13.4 0.0 collective-permute-done.4.even_c
  13.4 0.0 collective-permute-done.3.odd_b
  13.4 0.0 collective-permute-done.2.even_b
  13.4 0.0 collective-permute-done.5.odd_c
  13.4 19.5 %last_blocks.1 = bf16[128,4096]{1,0:T(8,128)(2,1)} custom-call(bf16[128,4096]{1,0:T(8,128)(2,1)S(1)} %get-tuple-element.14.q_ref, f32[3,8,128]{2,1,0:T(8,128)S(1)} %get-tuple-element.15.pen_ref, f32[4,1024,128]{2,1,0:T(8,128)S(1)} %get-tuple-element.18.out_in, f32[4,1024,128]{2,1,0:T(8,128)S(1)} %get-tuple-element.19.total_in, ...), custom_call_target="tpu_custom_call" | custom-call | tf_op jit(solution)/shard_map/last_blocks/pallas_call | solution.py:264
Async XLA Ops:
  1.0 9.2 %collective-permute-start.1 = (bf16[256,512]{1,0:T(8,128)(2,1)S(1)}, bf16[256,512]{1,0:T(8,128)(2,1)S(1)}, u32[]{:S(2)}, u32[]{:S(2)}) collective-permute-start(bf16[256,512]{1,0:T(8,128)(2,1)S(1)} %pack.1.kv_ref.own_ref), channel_id=1, source_target_pairs={{0,8},{1,3},{2,10},{3,5},{4,12},{5,7},{6,1},{7,9},{8,0},{9,11},{10... | collective-permute-start | bytes 786440 | tf_op jit(solution)/shard_map/ppermute | solution.py:224
  3.1 7.8 %collective-permute-start = (bf16[256,512]{1,0:T(8,128)(2,1)S(1)}, bf16[256,512]{1,0:T(8,128)(2,1)S(1)}, u32[]{:S(2)}, u32[]{:S(2)}) collective-permute-start(bf16[256,512]{1,0:T(8,128)(2,1)S(1)} %pack.1.kv_ref.own_ref), channel_id=1, source_target_pairs={{0,2},{1,9},{2,4},{3,11},{4,6},{5,13},{6,8},{7,0},{8,10},{9,1},{10... | collective-permute-start | bytes 786440 | tf_op jit(solution)/shard_map/ppermute | solution.py:224
  4.4 9.0 %collective-permute-start.3 = (bf16[256,512]{1,0:T(8,128)(2,1)S(1)}, bf16[256,512]{1,0:T(8,128)(2,1)S(1)}, u32[]{:S(2)}, u32[]{:S(2)}) collective-permute-start(bf16[256,512]{1,0:T(8,128)(2,1)S(1)} %pack.1.kv_ref.own_ref), channel_id=1, source_target_pairs={{0,1},{1,0},{2,3},{3,2},{4,5},{5,4},{6,7},{7,6},{8,9},{9,8},{10,11... | collective-permute-start | bytes 786440 | tf_op jit(solution)/shard_map/ppermute | solution.py:224
  8.3 5.1 %collective-permute-start.4 = (bf16[256,512]{1,0:T(8,128)(2,1)S(1)}, bf16[256,512]{1,0:T(8,128)(2,1)S(1)}, u32[]{:S(2)}, u32[]{:S(2)}) collective-permute-start(bf16[256,512]{1,0:T(8,128)(2,1)S(1)} %pack.1.kv_ref.own_ref), channel_id=1, source_target_pairs={{0,1},{1,4},{2,3},{3,6},{4,0},{5,8},{6,2},{7,10},{8,9},{9,12},{10,... | collective-permute-start | bytes 786440 | tf_op jit(solution)/shard_map/ppermute | solution.py:224
  10.2 3.2 %collective-permute-start.2 = (bf16[256,512]{1,0:T(8,128)(2,1)S(1)}, bf16[256,512]{1,0:T(8,128)(2,1)S(1)}, u32[]{:S(2)}, u32[]{:S(2)}) collective-permute-start(bf16[256,512]{1,0:T(8,128)(2,1)S(1)} %collective-permute-done.1.odd_a), channel_id=1, source_target_pairs={{0,1},{1,0},{2,3},{3,2},{4,5},{5,4},{6,7},{7,6},{8,9},{9,8},{10,11... | collective-permute-start | bytes 786440 | tf_op jit(solution)/shard_map/ppermute | solution.py:224
  10.9 2.5 %collective-permute-start.5 = (bf16[256,512]{1,0:T(8,128)(2,1)S(1)}, bf16[256,512]{1,0:T(8,128)(2,1)S(1)}, u32[]{:S(2)}, u32[]{:S(2)}) collective-permute-start(bf16[256,512]{1,0:T(8,128)(2,1)S(1)} %collective-permute-done.even_a), channel_id=1, source_target_pairs={{0,1},{1,0},{2,3},{3,2},{4,5},{5,4},{6,7},{7,6},{8,9},{9,8},{10,11... | collective-permute-start | bytes 786440 | tf_op jit(solution)/shard_map/ppermute | solution.py:224
where the time goes:
time: 33.1 us; the launch traced here: 32.9 us
  Pallas kernels  24.4 us (74%)
  starting transfers between devices  6.99 us (21%)
  waiting for transfers between devices  1.54 us (5%)
    pallas_call x1, Pallas kernels, on_device(): pl.pallas_call(functools.partial(last_kernel, groups, size), out_shape=ja...  19.5 us
    ppermute x6, starting transfers between devices, move(): return lax.ppermute(block, 'ctx', route)  6.99 us
    pallas_call x1, Pallas kernels, own(): pl.pallas_call(functools.partial(own_kernel, groups, size), out_shape=(ru...  2.66 us
    ppermute x6, waiting for transfers between devices, move(): return lax.ppermute(block, 'ctx', route)  1.54 us
    pallas_call x1, Pallas kernels, on_device(): pl.pallas_call(functools.partial(middle_kernel, groups, size), out_shape=...  1.19 us
    pallas_call x1, Pallas kernels, on_device(): pl.pallas_call(pack_kernel, out_shape=packed, in_specs=[HBM, HBM], out_sp...  0.98 us
  transfers between devices with their start and end apart: 6, of which 2 were waited for; matrix products, arithmetic and copies ran while one was open for 0% of the time, Pallas kernels for 12%

commit v1 on v0

v1 whole, which is shorter than its diff:
```python
import functools
import math

import jax
import jax.numpy as jnp
from jax import lax
from jax.experimental import pallas as pl
from jax.experimental.pallas import tpu as pltpu
from jax.sharding import PartitionSpec as P

HD = 128
BLK = 128
NEG = -1e30
LOW, HIGH = 1e-25, 1e35
EXP2_SCALE = math.log2(math.e) / math.sqrt(HD)
F32 = jnp.float32
BF16 = jnp.bfloat16
VMEM = pl.BlockSpec(memory_space=pltpu.VMEM)
HBM = pl.BlockSpec(memory_space=pltpu.HBM)
PARAMS = pltpu.CompilerParams(vmem_limit_bytes=40 * 1024 * 1024)


def dot_nt(a, b):
    return lax.dot_general(a, b, (((1,), (1,)), ((), ())), preferred_element_type=F32)


def dot_nn(a, b):
    return lax.dot_general(a, b, (((1,), (0,)), ((), ())), preferred_element_type=F32)


def cut(index, width=HD):
    return slice(index * width, (index + 1) * width)


def group_queries(q_ref, group, size):
    return jnp.concatenate([q_ref[:, cut(group * size + h)] for h in range(size)], axis=0)


def key_head(ref, group):
    return ref[:BLK, cut(group)]


def value_head(ref, group):
    return ref[BLK:, cut(group)]


def penalty(docs_ref, position, distance):
    source = position - distance
    same = docs_ref[jnp.maximum(source, 0)] == docs_ref[position]
    return jnp.where((source >= 0) & same, 0.0, -NEG).astype(F32)


def pack_kernel(k_hbm, v_hbm, kv_ref, sems):
    copies = [
        pltpu.make_async_copy(k_hbm, kv_ref.at[:BLK], sems.at[0]),
        pltpu.make_async_copy(v_hbm, kv_ref.at[BLK:], sems.at[1]),
    ]
    for copy in copies:
        copy.start()
    for copy in copies:
        copy.wait()


def load_queries(groups, size, q_hbm, q_ref, sems):
    spans = [cut(g, size * HD) for g in range(groups)]
    return [pltpu.make_async_copy(q_hbm.at[:, at], q_ref.at[:, at], sems.at[g]) for g, at in enumerate(spans)]


def own_blocks(size, some, q_ref, kv_ref, out_ref, total_ref, before=lambda g: None):
    row = lax.broadcasted_iota(jnp.int32, (BLK, BLK), 0)
    col = lax.broadcasted_iota(jnp.int32, (BLK, BLK), 1)
    bias = jnp.concatenate([jnp.where(col <= row, 0.0, NEG).astype(F32)] * size, axis=0)
    for g in some:
        before(g)
        scores = dot_nt(group_queries(q_ref, g, size), key_head(kv_ref, g))
        weights = jnp.exp2(scores * EXP2_SCALE + bias)
        total_ref[g] = weights
        out_ref[g] = dot_nn(weights.astype(BF16), value_head(kv_ref, g))


def own_kernel(groups, size, some, docs_hbm, q_hbm, kv_ref, out_ref, total_ref, pen_ref, q_ref, docs_ref, sems):
    docs_copy = pltpu.make_async_copy(docs_hbm, docs_ref, sems.at[groups])
    copies = load_queries(groups, size, q_hbm, q_ref, sems)
    for copy in copies + [docs_copy]:
        copy.start()
    own_blocks(size, some, q_ref, kv_ref, out_ref, total_ref, lambda g: copies[g].wait())
    for g in range(groups):
        if g not in some:
            copies[g].wait()
    docs_copy.wait()
    for i, distance in enumerate((2, 1, 3)):
        pen_ref[i] = jnp.full((8, HD), penalty(docs_ref, lax.axis_index("ctx"), distance), F32)


def rest_kernel(size, some, q_ref, kv_ref, out_in, total_in, out_ref, total_ref):
    own_blocks(size, some, q_ref, kv_ref, out_ref, total_ref)


def weigh(scores, pen):
    return jnp.exp2(scores * EXP2_SCALE - pen)


def add_blocks(queries, blocks, pens, group, out, total):
    scores = dot_nt(queries, jnp.concatenate([key_head(x, group) for x in blocks], axis=0))
    weights = [weigh(scores[:, cut(i)], pen) for i, pen in enumerate(pens)]
    rounded = jnp.concatenate([w.astype(BF16) for w in weights], axis=1)
    values = jnp.concatenate([value_head(x, group) for x in blocks], axis=0)
    return out + dot_nn(rounded, values), total + functools.reduce(jnp.add, weights)


def add_kernel(groups, size, q_ref, pen_ref, odd_a, out_in, total_in, out_ref, total_ref):
    @pl.when(lax.rem(lax.axis_index("ctx"), 2) == 1)
    def _():
        for g in range(groups):
            out_ref[g], total_ref[g] = add_blocks(
                group_queries(q_ref, g, size), [odd_a], [pen_ref[0][:1]], g, out_in[g], total_in[g]
            )


def finish(size, g, out, total, result_ref):
    row_total = jnp.sum(total, axis=1, keepdims=True)
    result = (out / row_total).astype(BF16)
    for h in range(size):
        result_ref[:, cut(g * size + h)] = result[cut(h, BLK)]
    return row_total


def note_extremes(row_totals, range_ref):
    low = functools.reduce(jnp.minimum, row_totals)
    high = functools.reduce(jnp.maximum, row_totals)
    range_ref[0] = jnp.full((8, HD), jnp.min(low), F32)
    range_ref[1] = jnp.full((8, HD), jnp.max(high), F32)


def even_kernel(groups, size, q_ref, pen_ref, even_a, even_b, out_in, total_in, out_ref, total_ref, out_hbm, range_ref, result_ref, sem):
    position = lax.axis_index("ctx")
    range_ref[...] = jnp.ones_like(range_ref)

    @pl.when((lax.rem(position, 2) == 0) & (position > 0))
    def _():
        pens = [pen_ref[i][:1] for i in (0, 1)]
        for g in range(groups):
            out_ref[g], total_ref[g] = add_blocks(
                group_queries(q_ref, g, size), [even_a, even_b], pens, g, out_in[g], total_in[g]
            )

    @pl.when(position == 0)
    def _():
        note_extremes([finish(size, g, out_in[g], total_in[g], result_ref) for g in range(groups)], range_ref)
        copy = pltpu.make_async_copy(result_ref, out_hbm, sem)
        copy.start()
        copy.wait()


def last_kernel(
    groups, size, q_ref, pen_ref, out_in, total_in, odd_b, odd_c, even_c,
    own_ref, even_a, odd_a, even_b, early_range, _, out_hbm, result_ref, range_ref, sems,
):
    position = lax.axis_index("ctx")
    odd = lax.rem(position, 2) == 1
    copies = []
    for g in range(groups):
        at = cut(g, size * HD)
        copies.append(pltpu.make_async_copy(result_ref.at[:, at], out_hbm.at[:, at], sems.at[g]))
    range_ref[...] = early_range[...]

    def whole(blocks, indices):
        pens = [pen_ref[i][:1] for i in indices]
        row_totals = []
        for g in range(groups):
            out, total = add_blocks(group_queries(q_ref, g, size), blocks, pens, g, out_in[g], total_in[g])
            row_totals.append(finish(size, g, out, total, result_ref))
            copies[g].start()
        note_extremes(row_totals, range_ref)

    @pl.when(jnp.logical_not(odd) & (position > 0))
    def _():
        whole([even_c], [2])

    @pl.when(odd)
    def _():
        whole([odd_b, odd_c], [1, 2])

    safe = (jnp.min(range_ref[0]) > LOW) & (jnp.max(range_ref[1]) < HIGH)

    @pl.when(position > 0)
    def _():
        for copy in copies:
            copy.wait()

    @pl.when(jnp.logical_not(safe))
    def _():
        row = lax.broadcasted_iota(jnp.int32, (BLK, BLK), 0)
        col = lax.broadcasted_iota(jnp.int32, (BLK, BLK), 1)
        biases = [jnp.where(col <= row, 0.0, NEG).astype(F32)] + [-pen_ref[i][:1] for i in range(3)]
        pairs = ((even_a, odd_a), (even_b, odd_b), (even_c, odd_c))
        for g in range(groups):
            keys, values = (
                [part(own_ref, g)] + [jnp.where(odd, part(y, g), part(x, g)) for x, y in pairs]
                for part in (key_head, value_head)
            )

            def one_head(h, _):
                at = pl.ds(pl.multiple_of((g * size + h) * HD, HD), HD)
                queries = q_ref[:, at]
                scores = [dot_nt(queries, x) + bias for x, bias in zip(keys, biases)]
                top = functools.reduce(jnp.maximum, [jnp.max(x, axis=1, keepdims=True) for x in scores])
                weights = [jnp.exp2((x - top) * EXP2_SCALE) for x in scores]
                total = sum(jnp.sum(w, axis=1, keepdims=True) for w in weights)
                product = sum(dot_nn(w.astype(BF16), x) for w, x in zip(weights, values))
                result_ref[:, at] = (product / total).astype(BF16)
                return 0

            lax.fori_loop(0, size, one_head, 0)
        store = pltpu.make_async_copy(result_ref, out_hbm, sems.at[0])
        store.start()
        store.wait()


def routes(n):
    step = n // 4
    forward = []
    for parity in (0, 1):
        route = {i: i + 2 for i in range(parity, n - 2, 2)}
        last = n - 2 + parity
        chain = [last, last ^ 1] + [(last ^ 1) - step * k for k in range(1, 4)] + [parity]
        route.update(zip(chain, chain[1:]))
        route.update({i: i ^ step for i in range(1 - parity, n, 2) if i not in route})
        forward.append(sorted(route.items()))
    across = {i: i + 3 for i in range(1, n - 3, 2)}
    for start, end in ((n - 3, 0), (n - 1, 2)):
        at = start
        for place in [start - step * (k + 1) for k in range(3)] + [end]:
            across[at] = place
            at = place - 1
    across.update({i: i + 1 for i in range(0, n, 2) if i not in across})
    swap = [(i, i ^ 1) for i in range(n)]
    return forward[0], forward[1], sorted(across.items()), swap


def in_hbm(array):
    return pltpu.with_memory_space_constraint(array, pltpu.HBM)


def after(value, *others):
    return lax.optimization_barrier((value, *others))[0]


def on_device(queries, keys, values, docs):
    row_count, width = keys.shape
    groups = width // HD
    size = queries.shape[1] // width
    rows = size * BLK
    n = lax.axis_size("ctx")
    assert row_count == BLK and n % 8 == 0
    even_on, odd_on, across, swap = routes(n)
    work = groups * rows * BLK * HD * 4
    cost = pl.CostEstimate(flops=0, bytes_accessed=0, transcendentals=0)
    packed = jax.ShapeDtypeStruct((2 * BLK, width), BF16)
    running = jax.ShapeDtypeStruct((groups, rows, HD), F32)
    extremes = jax.ShapeDtypeStruct((2, 8, HD), F32)
    result = jax.ShapeDtypeStruct(queries.shape, BF16)
    dma = pltpu.SemaphoreType.DMA

    def move(block, route):
        return lax.ppermute(block, "ctx", route)

    def own(block):
        some = tuple(range(groups))[:4]
        return pl.pallas_call(
            functools.partial(own_kernel, groups, size, some),
            out_shape=(running,) * 2 + (jax.ShapeDtypeStruct((3, 8, HD), F32), jax.ShapeDtypeStruct(queries.shape, BF16)),
            in_specs=[HBM, HBM, VMEM],
            out_specs=(VMEM,) * 4,
            scratch_shapes=[pltpu.SMEM(docs.shape, jnp.int32), dma((groups + 1,))],
            compiler_params=PARAMS,
            cost_estimate=cost,
            name="own_block",
        )(in_hbm(docs), in_hbm(queries), block)

    def rest(local, block, out, total):
        some = tuple(range(groups))[4:]
        return pl.pallas_call(
            functools.partial(rest_kernel, size, some),
            out_shape=(running,) * 2,
            in_specs=[VMEM] * 4,
            out_specs=(VMEM,) * 2,
            input_output_aliases={2: 0, 3: 1},
            compiler_params=PARAMS,
            cost_estimate=cost,
            name="own_rest",
        )(local, block, out, total)

    def add_odd(local, pen, out, total, odd_a):
        return pl.pallas_call(
            functools.partial(add_kernel, groups, size),
            out_shape=(running,) * 2,
            in_specs=[VMEM] * 5,
            out_specs=(VMEM,) * 2,
            input_output_aliases={3: 0, 4: 1},
            compiler_params=PARAMS,
            cost_estimate=cost,
            name="odd_blocks",
        )(local, pen, odd_a, out, total)

    def add_even(local, pen, out, total, even_a, even_b):
        return pl.pallas_call(
            functools.partial(even_kernel, groups, size),
            out_shape=(running, running, result, extremes),
            in_specs=[VMEM] * 6,
            out_specs=(VMEM, VMEM, HBM, VMEM),
            input_output_aliases={4: 0, 5: 1},
            scratch_shapes=[pltpu.VMEM(result.shape, BF16), dma(())],
            compiler_params=PARAMS,
            cost_estimate=cost,
            name="even_blocks",
        )(local, pen, even_a, even_b, out, total)

    block = pl.pallas_call(
        pack_kernel,
        out_shape=packed,
        in_specs=[HBM, HBM],
        out_specs=VMEM,
        scratch_shapes=[dma((2,))],
        compiler_params=PARAMS,
        name="pack",
    )(in_hbm(keys), in_hbm(values))
    odd_a = move(block, odd_on)
    even_a = move(block, even_on)
    out, total, pen, local = own(block)
    even_c = move(after(block, pen), across)
    odd_b = move(after(block, pen), swap)
    out, total = add_odd(local, pen, out, total, odd_a)
    even_b = move(after(odd_a, out), swap)
    odd_c = move(after(even_a, out), swap)
    out, total, early, early_range = add_even(local, pen, out, total, even_a, even_b)
    return pl.pallas_call(
        functools.partial(last_kernel, groups, size),
        out_shape=result,
        in_specs=[VMEM] * 12 + [HBM],
        out_specs=HBM,
        input_output_aliases={12: 0},
        scratch_shapes=[pltpu.VMEM(result.shape, BF16), pltpu.VMEM(extremes.shape, F32), dma((groups,))],
        compiler_params=PARAMS,
        cost_estimate=cost,
        name="last_blocks",
    )(
        local, pen, out, total, odd_b, odd_c, even_c, block, even_a, odd_a, even_b,
        early_range, in_hbm(early),
    )


def solution(mesh):
    return jax.shard_map(
        on_device,
        mesh=mesh,
        in_specs=(
            P(("seq", "ctx"), None),
            P(("seq", "ctx"), None),
            P(("seq", "ctx"), None),
            P("seq"),
        ),
        out_specs=P(("seq", "ctx"), None),
        check_vma=False,
    )
```

time: 33.1 us -> 33.2 us (level)
  starting transfers between devices: 6.99 us -> 5.85 us
  waiting for transfers between devices: 1.54 us -> 2.62 us
    ppermute x6, starting transfers between devices: 6.99 us -> 5.85 us  [move(): return lax.ppermute(block, 'ctx', route)]
    ppermute x6, waiting for transfers between devices: 1.54 us -> 2.62 us  [move(): return lax.ppermute(block, 'ctx', route)]
    pallas_call x3 -> x4, Pallas kernels: 23.4 us -> 23.5 us  [the longest x1 19.7 us: on_device(): pl.pallas_call(functools.partial(last_kernel, groups, size), out_shape=re...]
  transfers between devices with their start and end apart: 6 -> 6, of which waited for: 2 -> 3; matrix products, arithmetic and copies ran while one was open for 0% -> 0% of each run, Pallas kernels for 12% -> 12%
where the time goes in v1:
time: 33.2 us; the launch traced here: 33.1 us
  Pallas kernels  24.5 us (74%)
  starting transfers between devices  5.85 us (18%)
  waiting for transfers between devices  2.62 us (8%)
    pallas_call x1, Pallas kernels, on_device(): pl.pallas_call(functools.partial(last_kernel, groups, size), out_shape=re...  19.7 us
    ppermute x6, starting transfers between devices, move(): return lax.ppermute(block, 'ctx', route)  5.85 us
    pallas_call x1, Pallas kernels, own(): pl.pallas_call(functools.partial(own_kernel, groups, size, some), out_sha...  2.67 us
    ppermute x6, waiting for transfers between devices, move(): return lax.ppermute(block, 'ctx', route)  2.62 us
    pallas_call x1, Pallas kernels, add_odd(): pl.pallas_call(functools.partial(add_kernel, groups, size), out_shape=(ru...  1.17 us
    pallas_call x1, Pallas kernels, on_device(): pl.pallas_call(pack_kernel, out_shape=packed, in_specs=[HBM, HBM], out_sp...  0.98 us
  transfers between devices with their start and end apart: 6, of which 3 were waited for; matrix products, arithmetic and copies ran while one was open for 0% of the time, Pallas kernels for 12%

profile of v1, /device:TPU:1, one launch (start us, length us, event | category | flops | bytes accessed | tf_op | source)
XLA Modules:
  0.0 33.1 jit_solution(4174610399726500177)
XLA Ops:
  0.0 1.0 %pack.1.kv_ref.own_ref = bf16[256,512]{1,0:T(8,128)(2,1)S(1)} custom-call(bf16[128,512]{1,0:T(8,128)(2,1)} %k_hbm.1, bf16[128,512]{1,0:T(8,128)(2,1)} %v_hbm.1), custom_call_target="tpu_custom_call" | custom-call | tf_op jit(solution)/shard_map/pack/pallas_call | solution.py:319
  1.0 2.1 %collective-permute-start.1 = (bf16[256,512]{1,0:T(8,128)(2,1)S(1)}, bf16[256,512]{1,0:T(8,128)(2,1)S(1)}, u32[]{:S(2)}, u32[]{:S(2)}) collective-permute-start(bf16[256,512]{1,0:T(8,128)(2,1)S(1)} %pack.1.kv_ref.own_ref), channel_id=1, source_target_pairs={{0,8},{1,3},{2,10},{3,5},{4,12},{5,7},{6,1},{7,9},{8,0},{9,11},{10... | collective-permute-start | bytes 786440 | tf_op jit(solution)/shard_map/ppermute | solution.py:266
  3.1 1.3 %collective-permute-start = (bf16[256,512]{1,0:T(8,128)(2,1)S(1)}, bf16[256,512]{1,0:T(8,128)(2,1)S(1)}, u32[]{:S(2)}, u32[]{:S(2)}) collective-permute-start(bf16[256,512]{1,0:T(8,128)(2,1)S(1)} %pack.1.kv_ref.own_ref), channel_id=1, source_target_pairs={{0,2},{1,9},{2,4},{3,11},{4,6},{5,13},{6,8},{7,0},{8,10},{9,1},{10... | collective-permute-start | bytes 786440 | tf_op jit(solution)/shard_map/ppermute | solution.py:266
  4.4 2.7 %own_block.1 = (f32[4,1024,128]{2,1,0:T(8,128)S(1)}, f32[4,1024,128]{2,1,0:T(8,128)S(1)}, f32[3,8,128]{2,1,0:T(8,128)S(1)}, bf16[128,4096]{1,0:T(8,128)(2,1)S(1)}) custom-call(s32[32]{0:T(128)} %docs_hbm.1, bf16[128,4096]{1,0:T(8,128)(2,1)} %q_hbm.1, bf16[256,512]{1,0:T(8,128)(2,1)S(1)} %pack.1.kv_ref.own_ref), custom_call_target="tpu_custom_call" | custom-call | tf_op jit(solution)/shard_map/own_block/pallas_call | solution.py:270
  7.1 1.3 %collective-permute-start.3 = (bf16[256,512]{1,0:T(8,128)(2,1)S(1)}, bf16[256,512]{1,0:T(8,128)(2,1)S(1)}, u32[]{:S(2)}, u32[]{:S(2)}) collective-permute-start(bf16[256,512]{1,0:T(8,128)(2,1)S(1)} %pack.1.kv_ref.own_ref), channel_id=1, source_target_pairs={{0,1},{1,0},{2,3},{3,2},{4,5},{5,4},{6,7},{7,6},{8,9},{9,8},{10,11... | collective-permute-start | bytes 786440 | tf_op jit(solution)/shard_map/ppermute | solution.py:266
  8.4 0.4 %collective-permute-start.5 = (bf16[256,512]{1,0:T(8,128)(2,1)S(1)}, bf16[256,512]{1,0:T(8,128)(2,1)S(1)}, u32[]{:S(2)}, u32[]{:S(2)}) collective-permute-start(bf16[256,512]{1,0:T(8,128)(2,1)S(1)} %pack.1.kv_ref.own_ref), channel_id=1, source_target_pairs={{0,1},{1,4},{2,3},{3,6},{4,0},{5,8},{6,2},{7,10},{8,9},{9,12},{10,... | collective-permute-start | bytes 786440 | tf_op jit(solution)/shard_map/ppermute | solution.py:266
  8.8 1.5 %collective-permute-done.1.odd_a = bf16[256,512]{1,0:T(8,128)(2,1)S(1)} collective-permute-done((bf16[256,512]{1,0:T(8,128)(2,1)S(1)}, bf16[256,512]{1,0:T(8,128)(2,1)S(1)}, u32[]{:S(2)}, u32[]{:S(2)}) %collective-permute-start.1) | collective-permute-done | bytes 262176 | tf_op jit(solution)/shard_map/ppermute | solution.py:266
  10.2 1.2 %odd_blocks.1 = (f32[4,1024,128]{2,1,0:T(8,128)S(1)}, f32[4,1024,128]{2,1,0:T(8,128)S(1)}) custom-call(bf16[128,4096]{1,0:T(8,128)(2,1)S(1)} %get-tuple-element.18.q_ref, f32[3,8,128]{2,1,0:T(8,128)S(1)} %get-tuple-element.19.pen_ref, bf16[256,512]{1,0:T(8,128)(2,1)S(1)} %collective-permute-done.1.odd_a, ...), custom_call_target="tpu_custom_call", output_to_operand_aliasing={{0}: (3, {}), {1}: (4, {})} | custom-call | tf_op jit(solution)/shard_map/odd_blocks/pallas_call | solution.py:295
  11.4 0.1 collective-permute-start.2
  11.5 0.0 collective-permute-done.even_a
  11.5 0.7 %collective-permute-start.4 = (bf16[256,512]{1,0:T(8,128)(2,1)S(1)}, bf16[256,512]{1,0:T(8,128)(2,1)S(1)}, u32[]{:S(2)}, u32[]{:S(2)}) collective-permute-start(bf16[256,512]{1,0:T(8,128)(2,1)S(1)} %collective-permute-done.even_a), channel_id=1, source_target_pairs={{0,1},{1,0},{2,3},{3,2},{4,5},{5,4},{6,7},{7,6},{8,9},{9,8},{10,11... | collective-permute-start | bytes 786440 | tf_op jit(solution)/shard_map/ppermute | solution.py:266
  12.2 0.8 %collective-permute-done.2.even_b = bf16[256,512]{1,0:T(8,128)(2,1)S(1)} collective-permute-done((bf16[256,512]{1,0:T(8,128)(2,1)S(1)}, bf16[256,512]{1,0:T(8,128)(2,1)S(1)}, u32[]{:S(2)}, u32[]{:S(2)}) %collective-permute-start.2) | collective-permute-done | bytes 262176 | tf_op jit(solution)/shard_map/ppermute | solution.py:266
  13.0 0.0 collective-permute-done.3.odd_b
  13.0 0.0 collective-permute-done.5.even_c
  13.0 0.3 %collective-permute-done.4.odd_c = bf16[256,512]{1,0:T(8,128)(2,1)S(1)} collective-permute-done((bf16[256,512]{1,0:T(8,128)(2,1)S(1)}, bf16[256,512]{1,0:T(8,128)(2,1)S(1)}, u32[]{:S(2)}, u32[]{:S(2)}) %collective-permute-start.4) | collective-permute-done | bytes 262176 | tf_op jit(solution)/shard_map/ppermute | solution.py:266
  13.4 19.7 %last_blocks.1 = bf16[128,4096]{1,0:T(8,128)(2,1)} custom-call(bf16[128,4096]{1,0:T(8,128)(2,1)S(1)} %get-tuple-element.18.q_ref, f32[3,8,128]{2,1,0:T(8,128)S(1)} %get-tuple-element.19.pen_ref, f32[4,1024,128]{2,1,0:T(8,128)S(1)} %get-tuple-element.25.out_in, f32[4,1024,128]{2,1,0:T(8,128)S(1)} %get-tuple-element.26.total_in, ...), custom_call_target="tpu_custom_call", output_to_operand_aliasing={{}: (12, {})} | custom-call | tf_op jit(solution)/shard_map/last_blocks/pallas_call | solution.py:337
  (1 shorter events, 0.0 us)
Async XLA Ops:
  1.0 9.2 %collective-permute-start.1 = (bf16[256,512]{1,0:T(8,128)(2,1)S(1)}, bf16[256,512]{1,0:T(8,128)(2,1)S(1)}, u32[]{:S(2)}, u32[]{:S(2)}) collective-permute-start(bf16[256,512]{1,0:T(8,128)(2,1)S(1)} %pack.1.kv_ref.own_ref), channel_id=1, source_target_pairs={{0,8},{1,3},{2,10},{3,5},{4,12},{5,7},{6,1},{7,9},{8,0},{9,11},{10... | collective-permute-start | bytes 786440 | tf_op jit(solution)/shard_map/ppermute | solution.py:266
  3.1 8.4 %collective-permute-start = (bf16[256,512]{1,0:T(8,128)(2,1)S(1)}, bf16[256,512]{1,0:T(8,128)(2,1)S(1)}, u32[]{:S(2)}, u32[]{:S(2)}) collective-permute-start(bf16[256,512]{1,0:T(8,128)(2,1)S(1)} %pack.1.kv_ref.own_ref), channel_id=1, source_target_pairs={{0,2},{1,9},{2,4},{3,11},{4,6},{5,13},{6,8},{7,0},{8,10},{9,1},{10... | collective-permute-start | bytes 786440 | tf_op jit(solution)/shard_map/ppermute | solution.py:266
  7.1 6.0 %collective-permute-start.3 = (bf16[256,512]{1,0:T(8,128)(2,1)S(1)}, bf16[256,512]{1,0:T(8,128)(2,1)S(1)}, u32[]{:S(2)}, u32[]{:S(2)}) collective-permute-start(bf16[256,512]{1,0:T(8,128)(2,1)S(1)} %pack.1.kv_ref.own_ref), channel_id=1, source_target_pairs={{0,1},{1,0},{2,3},{3,2},{4,5},{5,4},{6,7},{7,6},{8,9},{9,8},{10,11... | collective-permute-start | bytes 786440 | tf_op jit(solution)/shard_map/ppermute | solution.py:266
  8.4 4.7 %collective-permute-start.5 = (bf16[256,512]{1,0:T(8,128)(2,1)S(1)}, bf16[256,512]{1,0:T(8,128)(2,1)S(1)}, u32[]{:S(2)}, u32[]{:S(2)}) collective-permute-start(bf16[256,512]{1,0:T(8,128)(2,1)S(1)} %pack.1.kv_ref.own_ref), channel_id=1, source_target_pairs={{0,1},{1,4},{2,3},{3,6},{4,0},{5,8},{6,2},{7,10},{8,9},{9,12},{10,... | collective-permute-start | bytes 786440 | tf_op jit(solution)/shard_map/ppermute | solution.py:266
  11.4 1.6 %collective-permute-start.2 = (bf16[256,512]{1,0:T(8,128)(2,1)S(1)}, bf16[256,512]{1,0:T(8,128)(2,1)S(1)}, u32[]{:S(2)}, u32[]{:S(2)}) collective-permute-start(bf16[256,512]{1,0:T(8,128)(2,1)S(1)} %collective-permute-done.1.odd_a), channel_id=1, source_target_pairs={{0,1},{1,0},{2,3},{3,2},{4,5},{5,4},{6,7},{7,6},{8,9},{9,8},{10,11... | collective-permute-start | bytes 786440 | tf_op jit(solution)/shard_map/ppermute | solution.py:266
  11.5 1.9 %collective-permute-start.4 = (bf16[256,512]{1,0:T(8,128)(2,1)S(1)}, bf16[256,512]{1,0:T(8,128)(2,1)S(1)}, u32[]{:S(2)}, u32[]{:S(2)}) collective-permute-start(bf16[256,512]{1,0:T(8,128)(2,1)S(1)} %collective-permute-done.even_a), channel_id=1, source_target_pairs={{0,1},{1,0},{2,3},{3,2},{4,5},{5,4},{6,7},{7,6},{8,9},{9,8},{10,11... | collective-permute-start | bytes 786440 | tf_op jit(solution)/shard_map/ppermute | solution.py:266

commit v2 on v1

--- a/solution.py
+++ b/solution.py
@@ -13,6 +13,7 @@
 NEG = -1e30
 LOW, HIGH = 1e-25, 1e35
 EXP2_SCALE = math.log2(math.e) / math.sqrt(HD)
+OWN_UNIT, ADD_UNIT, LAST_UNIT, PACK_PARTS = 8, 8, 4, 4
 F32 = jnp.float32
 BF16 = jnp.bfloat16
 VMEM = pl.BlockSpec(memory_space=pltpu.VMEM)
@@ -32,8 +33,32 @@
     return slice(index * width, (index + 1) * width)
 
 
-def group_queries(q_ref, group, size):
-    return jnp.concatenate([q_ref[:, cut(group * size + h)] for h in range(size)], axis=0)
+def unit_queries(q_ref, size, unit):
+    g, first, count = unit
+    return jnp.concatenate([q_ref[:, cut(g * size + first + h)] for h in range(count)], axis=0)
+
+
+def unit_rows(unit):
+    return slice(unit[1] * BLK, (unit[1] + unit[2]) * BLK)
+
+
+def units_of(groups, size, count):
+    return [(g, first, count) for g in groups for first in range(0, size, count)]
+
+
+def in_turn(units, first, second):
+    for unit in units:
+        second(unit, first(unit))
+
+
+def staggered(units, first, second):
+    waiting = None
+    for unit in units:
+        ready = (unit, first(unit))
+        if waiting is not None:
+            second(*waiting)
+        waiting = ready
+    second(*waiting)
 
 
 def key_head(ref, group):
@@ -51,10 +76,13 @@
 
 
 def pack_kernel(k_hbm, v_hbm, kv_ref, sems):
-    copies = [
-        pltpu.make_async_copy(k_hbm, kv_ref.at[:BLK], sems.at[0]),
-        pltpu.make_async_copy(v_hbm, kv_ref.at[BLK:], sems.at[1]),
-    ]
+    copies = []
+    for first, hbm in ((0, k_hbm), (BLK, v_hbm)):
+        for part in range(PACK_PARTS):
+            rows = BLK // PACK_PARTS
+            source = hbm.at[cut(part, rows)]
+            target = kv_ref.at[pl.ds(first + part * rows, rows)]
+            copies.append(pltpu.make_async_copy(source, target, sems.at[len(copies)]))
     for copy in copies:
         copy.start()
     for copy in copies:
@@ -69,13 +97,21 @@
 def own_blocks(size, some, q_ref, kv_ref, out_ref, total_ref, before=lambda g: None):
     row = lax.broadcasted_iota(jnp.int32, (BLK, BLK), 0)
     col = lax.broadcasted_iota(jnp.int32, (BLK, BLK), 1)
-    bias = jnp.concatenate([jnp.where(col <= row, 0.0, NEG).astype(F32)] * size, axis=0)
-    for g in some:
-        before(g)
-        scores = dot_nt(group_queries(q_ref, g, size), key_head(kv_ref, g))
-        weights = jnp.exp2(scores * EXP2_SCALE + bias)
-        total_ref[g] = weights
-        out_ref[g] = dot_nn(weights.astype(BF16), value_head(kv_ref, g))
+    count = OWN_UNIT
+    bias = jnp.concatenate([jnp.where(col <= row, 0.0, NEG).astype(F32)] * count, axis=0)
+
+    def first(unit):
+        if unit[1] == 0:
+            before(unit[0])
+        scores = dot_nt(unit_queries(q_ref, size, unit), key_head(kv_ref, unit[0]))
+        return jnp.exp2(scores * EXP2_SCALE + bias)
+
+    def second(unit, weights):
+        g, rows = unit[0], unit_rows(unit)
+        total_ref[g, rows] = weights
+        out_ref[g, rows] = dot_nn(weights.astype(BF16), value_head(kv_ref, g))
+
+    staggered(units_of(some, size, count), first, second)
 
 
 def own_kernel(groups, size, some, docs_hbm, q_hbm, kv_ref, out_ref, total_ref, pen_ref, q_ref, docs_ref, sems):
@@ -100,28 +136,43 @@
     return jnp.exp2(scores * EXP2_SCALE - pen)
 
 
-def add_blocks(queries, blocks, pens, group, out, total):
-    scores = dot_nt(queries, jnp.concatenate([key_head(x, group) for x in blocks], axis=0))
-    weights = [weigh(scores[:, cut(i)], pen) for i, pen in enumerate(pens)]
-    rounded = jnp.concatenate([w.astype(BF16) for w in weights], axis=1)
-    values = jnp.concatenate([value_head(x, group) for x in blocks], axis=0)
-    return out + dot_nn(rounded, values), total + functools.reduce(jnp.add, weights)
+def add_blocks(run, groups, size, count, q_ref, blocks, pens, out_in, total_in, store):
+    def first(unit):
+        keys = jnp.concatenate([key_head(x, unit[0]) for x in blocks], axis=0)
+        scores = dot_nt(unit_queries(q_ref, size, unit), keys)
+        return [weigh(scores[:, cut(i)], pen) for i, pen in enumerate(pens)]
+
+    def second(unit, weights):
+        g, rows = unit[0], unit_rows(unit)
+        rounded = jnp.concatenate([w.astype(BF16) for w in weights], axis=1)
+        values = jnp.concatenate([value_head(x, g) for x in blocks], axis=0)
+        out = out_in[g, rows] + dot_nn(rounded, values)
+        store(unit, out, total_in[g, rows] + functools.reduce(jnp.add, weights))
+
+    run(units_of(range(groups), size, count), first, second)
+
+
+def keep(out_ref, total_ref):
+    def store(unit, out, total):
+        out_ref[unit[0], unit_rows(unit)] = out
+        total_ref[unit[0], unit_rows(unit)] = total
+
+    return store
 
 
 def add_kernel(groups, size, q_ref, pen_ref, odd_a, out_in, total_in, out_ref, total_ref):
     @pl.when(lax.rem(lax.axis_index("ctx"), 2) == 1)
     def _():
-        for g in range(groups):
-            out_ref[g], total_ref[g] = add_blocks(
-                group_queries(q_ref, g, size), [odd_a], [pen_ref[0][:1]], g, out_in[g], total_in[g]
-            )
-
-
-def finish(size, g, out, total, result_ref):
+        pens = [pen_ref[0][:1]]
+        add_blocks(in_turn, groups, size, ADD_UNIT, q_ref, [odd_a], pens, out_in, total_in, keep(out_ref, total_ref))
+
+
+def finish(size, unit, out, total, result_ref):
     row_total = jnp.sum(total, axis=1, keepdims=True)
     result = (out / row_total).astype(BF16)
-    for h in range(size):
-        result_ref[:, cut(g * size + h)] = result[cut(h, BLK)]
+    g, first, count = unit
+    for h in range(count):
+        result_ref[:, cut(g * size + first + h)] = result[cut(h, BLK)]
     return row_total
 
 
@@ -139,14 +190,12 @@
     @pl.when((lax.rem(position, 2) == 0) & (position > 0))
     def _():
         pens = [pen_ref[i][:1] for i in (0, 1)]
-        for g in range(groups):
-            out_ref[g], total_ref[g] = add_blocks(
-                group_queries(q_ref, g, size), [even_a, even_b], pens, g, out_in[g], total_in[g]
-            )
+        add_blocks(in_turn, groups, size, ADD_UNIT, q_ref, [even_a, even_b], pens, out_in, total_in, keep(out_ref, total_ref))
 
     @pl.when(position == 0)
     def _():
-        note_extremes([finish(size, g, out_in[g], total_in[g], result_ref) for g in range(groups)], range_ref)
+        whole = units_of(range(groups), size, size)
+        note_extremes([finish(size, u, out_in[u[0]], total_in[u[0]], result_ref) for u in whole], range_ref)
         copy = pltpu.make_async_copy(result_ref, out_hbm, sem)
         copy.start()
         copy.wait()
@@ -158,19 +207,23 @@
 ):
     position = lax.axis_index("ctx")
     odd = lax.rem(position, 2) == 1
-    copies = []
-    for g in range(groups):
-        at = cut(g, size * HD)
-        copies.append(pltpu.make_async_copy(result_ref.at[:, at], out_hbm.at[:, at], sems.at[g]))
+    units = units_of(range(groups), size, LAST_UNIT)
+    copies = {}
+    for n, unit in enumerate(units):
+        start = (unit[0] * size + unit[1]) * HD
+        at = slice(start, start + unit[2] * HD)
+        copies[unit] = pltpu.make_async_copy(result_ref.at[:, at], out_hbm.at[:, at], sems.at[n])
     range_ref[...] = early_range[...]
 
     def whole(blocks, indices):
         pens = [pen_ref[i][:1] for i in indices]
         row_totals = []
-        for g in range(groups):
-            out, total = add_blocks(group_queries(q_ref, g, size), blocks, pens, g, out_in[g], total_in[g])
-            row_totals.append(finish(size, g, out, total, result_ref))
-            copies[g].start()
+
+        def store(unit, out, total):
+            row_totals.append(finish(size, unit, out, total, result_ref))
+            copies[unit].start()
+
+        add_blocks(staggered, groups, size, LAST_UNIT, q_ref, blocks, pens, out_in, total_in, store)
         note_extremes(row_totals, range_ref)
 
     @pl.when(jnp.logical_not(odd) & (position > 0))
@@ -185,7 +238,7 @@
 
     @pl.when(position > 0)
     def _():
-        for copy in copies:
+        for copy in copies.values():
             copy.wait()
 
     @pl.when(jnp.logical_not(safe))
@@ -321,7 +374,7 @@
         out_shape=packed,
         in_specs=[HBM, HBM],
         out_specs=VMEM,
-        scratch_shapes=[dma((2,))],
+        scratch_shapes=[dma((2 * PACK_PARTS,))],
         compiler_params=PARAMS,
         name="pack",
     )(in_hbm(keys), in_hbm(values))
@@ -340,7 +393,7 @@
         in_specs=[VMEM] * 12 + [HBM],
         out_specs=HBM,
         input_output_aliases={12: 0},
-        scratch_shapes=[pltpu.VMEM(result.shape, BF16), pltpu.VMEM(extremes.shape, F32), dma((groups,))],
+        scratch_shapes=[pltpu.VMEM(result.shape, BF16), pltpu.VMEM(extremes.shape, F32), dma((groups * size // LAST_UNIT,))],
         compiler_params=PARAMS,
         cost_estimate=cost,
         name="last_blocks",

time: 33.2 us -> 33.3 us (level)
  transfers between devices with their start and end apart: 6 -> 6, of which waited for: 3 -> 3; matrix products, arithmetic and copies ran while one was open for 0% -> 0% of each run, Pallas kernels for 12% -> 11%
where the time goes in v2:
time: 33.3 us; the launch traced here: 33.1 us
  Pallas kernels  24.3 us (73%)
  starting transfers between devices  5.87 us (18%)
  waiting for transfers between devices  2.84 us (9%)
    pallas_call x1, Pallas kernels, on_device(): pl.pallas_call(functools.partial(last_kernel, groups, size), out_shape=re...  19.7 us
    ppermute x6, starting transfers between devices, move(): return lax.ppermute(block, 'ctx', route)  5.87 us
    ppermute x6, waiting for transfers between devices, move(): return lax.ppermute(block, 'ctx', route)  2.84 us
    pallas_call x1, Pallas kernels, own(): pl.pallas_call(functools.partial(own_kernel, groups, size, some), out_sha...  2.43 us
    pallas_call x1, Pallas kernels, add_odd(): pl.pallas_call(functools.partial(add_kernel, groups, size), out_shape=(ru...  1.17 us
    pallas_call x1, Pallas kernels, on_device(): pl.pallas_call(pack_kernel, out_shape=packed, in_specs=[HBM, HBM], out_sp...  0.94 us
  transfers between devices with their start and end apart: 6, of which 3 were waited for; matrix products, arithmetic and copies ran while one was open for 0% of the time, Pallas kernels for 11%

profile of v2, /device:TPU:1, one launch (start us, length us, event | category | flops | bytes accessed | tf_op | source)
XLA Modules:
  0.0 33.1 jit_solution(2082386675833457688)
XLA Ops:
  0.0 0.9 %pack.1.kv_ref.own_ref = bf16[256,512]{1,0:T(8,128)(2,1)S(1)} custom-call(bf16[128,512]{1,0:T(8,128)(2,1)} %k_hbm.1, bf16[128,512]{1,0:T(8,128)(2,1)} %v_hbm.1), custom_call_target="tpu_custom_call" | custom-call | tf_op jit(solution)/shard_map/pack/pallas_call | solution.py:372
  0.9 2.1 %collective-permute-start.1 = (bf16[256,512]{1,0:T(8,128)(2,1)S(1)}, bf16[256,512]{1,0:T(8,128)(2,1)S(1)}, u32[]{:S(2)}, u32[]{:S(2)}) collective-permute-start(bf16[256,512]{1,0:T(8,128)(2,1)S(1)} %pack.1.kv_ref.own_ref), channel_id=1, source_target_pairs={{0,8},{1,3},{2,10},{3,5},{4,12},{5,7},{6,1},{7,9},{8,0},{9,11},{10... | collective-permute-start | bytes 786440 | tf_op jit(solution)/shard_map/ppermute | solution.py:319
  3.0 1.3 %collective-permute-start = (bf16[256,512]{1,0:T(8,128)(2,1)S(1)}, bf16[256,512]{1,0:T(8,128)(2,1)S(1)}, u32[]{:S(2)}, u32[]{:S(2)}) collective-permute-start(bf16[256,512]{1,0:T(8,128)(2,1)S(1)} %pack.1.kv_ref.own_ref), channel_id=1, source_target_pairs={{0,2},{1,9},{2,4},{3,11},{4,6},{5,13},{6,8},{7,0},{8,10},{9,1},{10... | collective-permute-start | bytes 786440 | tf_op jit(solution)/shard_map/ppermute | solution.py:319
  4.3 2.4 %own_block.1 = (f32[4,1024,128]{2,1,0:T(8,128)S(1)}, f32[4,1024,128]{2,1,0:T(8,128)S(1)}, f32[3,8,128]{2,1,0:T(8,128)S(1)}, bf16[128,4096]{1,0:T(8,128)(2,1)S(1)}) custom-call(s32[32]{0:T(128)} %docs_hbm.1, bf16[128,4096]{1,0:T(8,128)(2,1)} %q_hbm.1, bf16[256,512]{1,0:T(8,128)(2,1)S(1)} %pack.1.kv_ref.own_ref), custom_call_target="tpu_custom_call" | custom-call | tf_op jit(solution)/shard_map/own_block/pallas_call | solution.py:323
  6.8 1.3 %collective-permute-start.3 = (bf16[256,512]{1,0:T(8,128)(2,1)S(1)}, bf16[256,512]{1,0:T(8,128)(2,1)S(1)}, u32[]{:S(2)}, u32[]{:S(2)}) collective-permute-start(bf16[256,512]{1,0:T(8,128)(2,1)S(1)} %pack.1.kv_ref.own_ref), channel_id=1, source_target_pairs={{0,1},{1,0},{2,3},{3,2},{4,5},{5,4},{6,7},{7,6},{8,9},{9,8},{10,11... | collective-permute-start | bytes 786440 | tf_op jit(solution)/shard_map/ppermute | solution.py:319
  8.1 0.4 %collective-permute-start.5 = (bf16[256,512]{1,0:T(8,128)(2,1)S(1)}, bf16[256,512]{1,0:T(8,128)(2,1)S(1)}, u32[]{:S(2)}, u32[]{:S(2)}) collective-permute-start(bf16[256,512]{1,0:T(8,128)(2,1)S(1)} %pack.1.kv_ref.own_ref), channel_id=1, source_target_pairs={{0,1},{1,4},{2,3},{3,6},{4,0},{5,8},{6,2},{7,10},{8,9},{9,12},{10,... | collective-permute-start | bytes 786440 | tf_op jit(solution)/shard_map/ppermute | solution.py:319
  8.5 1.7 %collective-permute-done.1.odd_a = bf16[256,512]{1,0:T(8,128)(2,1)S(1)} collective-permute-done((bf16[256,512]{1,0:T(8,128)(2,1)S(1)}, bf16[256,512]{1,0:T(8,128)(2,1)S(1)}, u32[]{:S(2)}, u32[]{:S(2)}) %collective-permute-start.1) | collective-permute-done | bytes 262176 | tf_op jit(solution)/shard_map/ppermute | solution.py:319
  10.2 1.2 %odd_blocks.1 = (f32[4,1024,128]{2,1,0:T(8,128)S(1)}, f32[4,1024,128]{2,1,0:T(8,128)S(1)}) custom-call(bf16[128,4096]{1,0:T(8,128)(2,1)S(1)} %get-tuple-element.18.q_ref, f32[3,8,128]{2,1,0:T(8,128)S(1)} %get-tuple-element.19.pen_ref, bf16[256,512]{1,0:T(8,128)(2,1)S(1)} %collective-permute-done.1.odd_a, ...), custom_call_target="tpu_custom_call", output_to_operand_aliasing={{0}: (3, {}), {1}: (4, {})} | custom-call | tf_op jit(solution)/shard_map/odd_blocks/pallas_call | solution.py:348
  11.4 0.1 collective-permute-start.2
  11.4 0.0 collective-permute-done.even_a
  11.4 0.7 %collective-permute-start.4 = (bf16[256,512]{1,0:T(8,128)(2,1)S(1)}, bf16[256,512]{1,0:T(8,128)(2,1)S(1)}, u32[]{:S(2)}, u32[]{:S(2)}) collective-permute-start(bf16[256,512]{1,0:T(8,128)(2,1)S(1)} %collective-permute-done.even_a), channel_id=1, source_target_pairs={{0,1},{1,0},{2,3},{3,2},{4,5},{5,4},{6,7},{7,6},{8,9},{9,8},{10,11... | collective-permute-start | bytes 786440 | tf_op jit(solution)/shard_map/ppermute | solution.py:319
  12.2 0.8 %collective-permute-done.2.even_b = bf16[256,512]{1,0:T(8,128)(2,1)S(1)} collective-permute-done((bf16[256,512]{1,0:T(8,128)(2,1)S(1)}, bf16[256,512]{1,0:T(8,128)(2,1)S(1)}, u32[]{:S(2)}, u32[]{:S(2)}) %collective-permute-start.2) | collective-permute-done | bytes 262176 | tf_op jit(solution)/shard_map/ppermute | solution.py:319
  13.0 0.0 collective-permute-done.3.odd_b
  13.0 0.0 collective-permute-done.5.even_c
  13.0 0.3 %collective-permute-done.4.odd_c = bf16[256,512]{1,0:T(8,128)(2,1)S(1)} collective-permute-done((bf16[256,512]{1,0:T(8,128)(2,1)S(1)}, bf16[256,512]{1,0:T(8,128)(2,1)S(1)}, u32[]{:S(2)}, u32[]{:S(2)}) %collective-permute-start.4) | collective-permute-done | bytes 262176 | tf_op jit(solution)/shard_map/ppermute | solution.py:319
  13.3 19.7 %last_blocks.1 = bf16[128,4096]{1,0:T(8,128)(2,1)} custom-call(bf16[128,4096]{1,0:T(8,128)(2,1)S(1)} %get-tuple-element.18.q_ref, f32[3,8,128]{2,1,0:T(8,128)S(1)} %get-tuple-element.19.pen_ref, f32[4,1024,128]{2,1,0:T(8,128)S(1)} %get-tuple-element.25.out_in, f32[4,1024,128]{2,1,0:T(8,128)S(1)} %get-tuple-element.26.total_in, ...), custom_call_target="tpu_custom_call", output_to_operand_aliasing={{}: (12, {})} | custom-call | tf_op jit(solution)/shard_map/last_blocks/pallas_call | solution.py:390
  (1 shorter events, 0.0 us)
Async XLA Ops:
  0.9 9.2 %collective-permute-start.1 = (bf16[256,512]{1,0:T(8,128)(2,1)S(1)}, bf16[256,512]{1,0:T(8,128)(2,1)S(1)}, u32[]{:S(2)}, u32[]{:S(2)}) collective-permute-start(bf16[256,512]{1,0:T(8,128)(2,1)S(1)} %pack.1.kv_ref.own_ref), channel_id=1, source_target_pairs={{0,8},{1,3},{2,10},{3,5},{4,12},{5,7},{6,1},{7,9},{8,0},{9,11},{10... | collective-permute-start | bytes 786440 | tf_op jit(solution)/shard_map/ppermute | solution.py:319
  3.0 8.4 %collective-permute-start = (bf16[256,512]{1,0:T(8,128)(2,1)S(1)}, bf16[256,512]{1,0:T(8,128)(2,1)S(1)}, u32[]{:S(2)}, u32[]{:S(2)}) collective-permute-start(bf16[256,512]{1,0:T(8,128)(2,1)S(1)} %pack.1.kv_ref.own_ref), channel_id=1, source_target_pairs={{0,2},{1,9},{2,4},{3,11},{4,6},{5,13},{6,8},{7,0},{8,10},{9,1},{10... | collective-permute-start | bytes 786440 | tf_op jit(solution)/shard_map/ppermute | solution.py:319
  6.8 6.2 %collective-permute-start.3 = (bf16[256,512]{1,0:T(8,128)(2,1)S(1)}, bf16[256,512]{1,0:T(8,128)(2,1)S(1)}, u32[]{:S(2)}, u32[]{:S(2)}) collective-permute-start(bf16[256,512]{1,0:T(8,128)(2,1)S(1)} %pack.1.kv_ref.own_ref), channel_id=1, source_target_pairs={{0,1},{1,0},{2,3},{3,2},{4,5},{5,4},{6,7},{7,6},{8,9},{9,8},{10,11... | collective-permute-start | bytes 786440 | tf_op jit(solution)/shard_map/ppermute | solution.py:319
  8.1 4.9 %collective-permute-start.5 = (bf16[256,512]{1,0:T(8,128)(2,1)S(1)}, bf16[256,512]{1,0:T(8,128)(2,1)S(1)}, u32[]{:S(2)}, u32[]{:S(2)}) collective-permute-start(bf16[256,512]{1,0:T(8,128)(2,1)S(1)} %pack.1.kv_ref.own_ref), channel_id=1, source_target_pairs={{0,1},{1,4},{2,3},{3,6},{4,0},{5,8},{6,2},{7,10},{8,9},{9,12},{10,... | collective-permute-start | bytes 786440 | tf_op jit(solution)/shard_map/ppermute | solution.py:319
  11.4 1.6 %collective-permute-start.2 = (bf16[256,512]{1,0:T(8,128)(2,1)S(1)}, bf16[256,512]{1,0:T(8,128)(2,1)S(1)}, u32[]{:S(2)}, u32[]{:S(2)}) collective-permute-start(bf16[256,512]{1,0:T(8,128)(2,1)S(1)} %collective-permute-done.1.odd_a), channel_id=1, source_target_pairs={{0,1},{1,0},{2,3},{3,2},{4,5},{5,4},{6,7},{7,6},{8,9},{9,8},{10,11... | collective-permute-start | bytes 786440 | tf_op jit(solution)/shard_map/ppermute | solution.py:319
  11.4 1.9 %collective-permute-start.4 = (bf16[256,512]{1,0:T(8,128)(2,1)S(1)}, bf16[256,512]{1,0:T(8,128)(2,1)S(1)}, u32[]{:S(2)}, u32[]{:S(2)}) collective-permute-start(bf16[256,512]{1,0:T(8,128)(2,1)S(1)} %collective-permute-done.even_a), channel_id=1, source_target_pairs={{0,1},{1,0},{2,3},{3,2},{4,5},{5,4},{6,7},{7,6},{8,9},{9,8},{10,11... | collective-permute-start | bytes 786440 | tf_op jit(solution)/shard_map/ppermute | solution.py:319
